TPU v7x, 32 devices: a whole 2x2x4 slice. The times are simulated.
32 devices in a mesh: tower: 2 (over y), narrow: 4 (over z), wide: 4 (over x, core).
Axes of the slice: x: 2, y: 2, z: 4, core: 2. Of those that a mesh axis runs over, the one named last changes fastest.
Arguments:
- features: bfloat16 [4, 8, 256, 2048], P('narrow', ('tower', 'wide')), may hold values from -6 to 6
- w_in: bfloat16 [2048, 4096], P(None, 'narrow'), may hold values from -0.125 to 0.125
- b_in: float32 [4096], P('narrow'), may hold values from -0.5 to 0.5
- w_out: bfloat16 [4096, 256], P('narrow'), may hold values from -0.09375 to 0.09375
- user_emb: bfloat16 [8192, 256], P('narrow'), as said below
- item_ids: int32 [4, 8, 256], P('narrow', ('tower', 'wide')), may hold values from 0 to 8191
Outputs:
- row_loss: float32 [8192], P('narrow')
- item_grad: float32 [4, 8, 256, 256], P('narrow', ('tower', 'wide'))
Inputs may be any that keep to these rules, and one draw needn't show every extreme that they name: `user_emb`: user embeddings.
All inputs are finite; a program needn't handle non-finite values.
Results may differ from a plain program's by a relative error of at most 0.024.
Values may be sent and summed in bfloat16 or wider, within the bound.
A program may use at most 64 MiB of HBM per device.

v0:
```python
import jax
import jax.numpy as jnp
from jax import lax
from jax.sharding import PartitionSpec as P

INV_TEMP = 4.0
EPS = 1e-06
NEG = -1e30


def unit_rows(embed):
    return embed * lax.rsqrt(jnp.sum(embed * embed, axis=1, keepdims=True) + EPS)


def block_scores(user, rid, rglob, vectors, col_ids, col_glob):
    scores = (
        lax.dot_general(user, vectors, (((1,), (1,)), ((), ())), preferred_element_type=jnp.float32)
        * INV_TEMP
    )
    diag = rglob[:, None] == col_glob[None, :]
    keep = (rid[:, None] != col_ids[None, :]) | diag
    return (scores, diag, keep)


def block_scores_cols(vectors, col_ids, col_glob, user, rid, rglob):
    scores = (
        lax.dot_general(vectors, user, (((1,), (1,)), ((), ())), preferred_element_type=jnp.float32)
        * INV_TEMP
    )
    diag = col_glob[:, None] == rglob[None, :]
    keep = (col_ids[:, None] != rid[None, :]) | diag
    return (scores, diag, keep)


def local(features, w_in, b_in, w_out, user_emb, item_ids):
    share = features.shape[2]
    width = features.shape[3]
    embed_width = w_out.shape[1]
    users_dev = user_emb.shape[0]
    groups = lax.axis_size("narrow")
    panel = groups * share
    gathered, gathered_ids = (
        lax.all_gather(features, "narrow", axis=0, tiled=True),
        lax.all_gather(item_ids, "narrow", axis=0, tiled=True),
    )
    rows_in = gathered.reshape(panel, width)
    col_ids = gathered_ids.reshape(panel)
    hidden = jax.nn.relu(jnp.dot(rows_in, w_in, preferred_element_type=jnp.float32) + b_in).astype(
        jnp.bfloat16
    )
    partial_embed = jnp.dot(hidden, w_out, preferred_element_type=jnp.float32)
    item_vec = unit_rows(lax.psum(partial_embed, "narrow")).astype(jnp.bfloat16)
    row_ids = lax.all_gather(item_ids, ("tower", "wide"), axis=1, tiled=True).reshape(users_dev)
    narrow_index = lax.axis_index("narrow")
    panel_index = lax.axis_index(("tower", "wide"))
    row_glob = narrow_index * users_dev + jnp.arange(users_dev, dtype=jnp.int32)
    column = jnp.arange(panel, dtype=jnp.int32)
    col_glob = column // share * users_dev + panel_index * share + column % share
    block = min(512, users_dev)
    count = users_dev // block
    users = user_emb.reshape(count, block, embed_width)
    rid_blocks = row_ids.reshape(count, block)
    rglob_blocks = row_glob.reshape(count, block)

    def local_stats(blk):
        user, rid, rglob = blk
        scores, diag, keep = block_scores(user, rid, rglob, item_vec, col_ids, col_glob)
        masked = jnp.where(keep, scores, NEG)
        top = jnp.max(masked, axis=1)
        mass = jnp.sum(jnp.where(keep, jnp.exp(scores - top[:, None]), 0.0), axis=1)
        pos = jnp.sum(jnp.where(diag, scores, 0.0), axis=1)
        return (top, mass, pos, masked.T)

    def local_stats_only(blk):
        top, mass, pos, masked = local_stats(blk)
        return (top, mass, pos)

    top, mass, pos = lax.map(local_stats_only, (users, rid_blocks, rglob_blocks))
    top = top.reshape(users_dev)
    mass = mass.reshape(users_dev)
    pos = pos.reshape(users_dev)
    global_top = lax.pmax(top, ("tower", "wide"))
    total, global_pos = lax.psum((mass * jnp.exp(top - global_top), pos), ("tower", "wide"))
    lse = global_top + jnp.log(total)
    row_loss = lse - global_pos
    lse_blocks = lse.reshape(count, block)

    def add_block(acc, blk):
        user, rid, rglob, lse_blk = blk
        scores, diag, keep = block_scores_cols(item_vec, col_ids, col_glob, user, rid, rglob)
        coef = (
            jnp.where(keep, jnp.exp(scores - lse_blk[None, :]), 0.0) - diag.astype(jnp.float32)
        ).astype(jnp.bfloat16)
        term = jnp.dot(coef, user, preferred_element_type=jnp.float32)
        return (acc + term, None)

    acc, unused = lax.scan(
        add_block,
        jnp.zeros((share * lax.axis_size("narrow"), embed_width), jnp.float32),
        (users, rid_blocks, rglob_blocks, lse_blocks),
    )
    own_grad = lax.psum_scatter(INV_TEMP * acc, "narrow", scatter_dimension=0, tiled=True)
    return (row_loss, own_grad.reshape(1, 1, share, embed_width))


def solution(mesh):
    return jax.shard_map(
        local,
        mesh=mesh,
        in_specs=(
            P("narrow", ("tower", "wide"), None, None),
            P(None, "narrow"),
            P("narrow"),
            P("narrow", None),
            P("narrow", None),
            P("narrow", ("tower", "wide"), None),
        ),
        out_specs=(P("narrow"), P("narrow", ("tower", "wide"), None, None)),
        check_vma=False,
    )
```

profile of v0, /device:TPU:0, one launch (start us, length us, event | category | flops | bytes accessed | tf_op | source)
XLA Modules:
  0.0 238.5 jit_solution(5663523277225741020)
XLA Ops:
  7.2 0.0 copy-start
  7.2 0.0 all-gather.2.cloned.1.call-start
  7.2 0.7 all-gather.2.cloned.1.call-update
  7.9 0.0 all-reduce.3.cloned.1.call-start
  8.0 85.1 %all-gather.2.cloned.1.call-done = bf16[4,1,256,2048]{3,2,1,0:T(8,128)(2,1)} async-done(((bf16[1,1,256,2048]{3,2,1,0:T(8,128)(2,1)}), bf16[4,1,256,2048]{3,2,1,0:T(8,128)(2,1)}) %all-gather.2.cloned.1.call-update) | async-done | bytes 4194320 | tf_op jit(solution)/shard_map/all_gather | solution.py:43
  93.1 0.0 copy-done
  93.1 0.0 copy-start.1
  93.1 9.6 %fusion.48 = f32[1024,256]{1,0:T(8,128)} fusion(bf16[1024,256]{1,0:T(8,128)(2,1)S(1)} %copy-done, f32[1024]{0:T(1024)} %param.12, bf16[1024,2048]{1,0:T(8,128)(2,1)} %bitcast.95, bf16[2048,1024]{1,0:T(8,128)(2,1)} %param.11), kind=kOutput, calls=%fused_computation.64 | convolution fusion | flops 4834983936 | bytes 9965568 | tf_op jit(solution)/shard_map/dot_general | solution.py:51
  102.7 0.0 copy-start.2
  102.7 0.0 all-reduce.3.cloned.1.call-update
  102.7 0.0 reduce-scatter.2.cloned.1.call-start
  102.8 0.0 copy-done.1
  102.8 9.0 %all_gather.9 = s32[1,8,256]{2,0,1:T(1,128)S(1)} all-gather(s32[1,1,256]{2,0,1:T(1,128)S(1)} %bitcast.94), channel_id=1, replica_groups=mesh['tower'=2,'narrow'=4,'wide'=4] {'tower','wide'}, dimensions={1}, use_global_device_ids=true | all-gather | bytes 9216 | tf_op jit(solution)/shard_map/all_gather | solution.py:53
  111.9 8.8 %all_gather.10 = s32[4,1,256]{2,1,0:T(1,128)S(1)} all-gather(s32[1,1,256]{2,1,0:T(1,128)S(1)} %copy-done.1), channel_id=1, replica_groups=mesh['tower'=2,'narrow'=4,'wide'=4] {'narrow'}, dimensions={0}, use_global_device_ids=true | all-gather | bytes 5120 | tf_op jit(solution)/shard_map/all_gather | solution.py:44
  120.7 32.6 %all-reduce.3.cloned.1.call-done = f32[1024,256]{1,0:T(8,128)} async-done(((f32[1024,256]{1,0:T(8,128)}), f32[1024,256]{1,0:T(8,128)}) %all-reduce.3.cloned.1.call-update) | async-done | bytes 1048592 | tf_op jit(solution)/shard_map/psum | solution.py:52
  153.3 1.4 multiply_reduce_fusion
  154.8 1.4 multiply_convert_fusion
  156.2 0.0 copy-done.2
  156.2 7.8 %while.26 = (s32[]{:T(128)}, f32[4,512]{1,0:T(4,128)S(1)}, f32[4,512]{1,0:T(4,128)S(1)}, f32[4,512]{1,0:T(4,128)S(1)}, s32[4,512]{1,0:T(4,128)S(1)}, /*index=5*/...) while((s32[]{:T(128)}, f32[4,512]{1,0:T(4,128)S(1)}, ...), condition=%wide.region_6.7_spmd.clone, body=%wide.region_2.6_spmd.clone.sunk | while | flops 276313600 | bytes 5038221 | solution.py:78
  156.2 0.7 select_reduce_fusion.3
  156.9 1.1 fusion.70
  158.0 0.1 dynamic_update_slice.17
  158.1 0.1 dynamic_update_slice.16
  158.2 0.7 select_reduce_fusion.3
  158.9 1.1 fusion.70
  160.0 0.1 dynamic_update_slice.17
  160.0 0.1 dynamic_update_slice.16
  160.1 0.7 select_reduce_fusion.3
  160.8 1.1 fusion.70
  162.0 0.1 dynamic_update_slice.17
  162.0 0.1 dynamic_update_slice.16
  162.1 0.7 select_reduce_fusion.3
  162.8 1.1 fusion.70
  163.9 0.1 dynamic_update_slice.17
  164.0 0.1 dynamic_update_slice.16
  164.0 14.1 %pmax.7 = f32[2048]{0:T(1024)S(1)} all-reduce(f32[2048]{0:T(1024)S(1)} %bitcast.84), channel_id=1, replica_groups=mesh['tower'=2,'narrow'=4,'wide'=4] {'tower','wide'}, use_global_device_ids=true, to_apply=%region_7.8 | all-reduce | flops 2048 | bytes 16384 | tf_op jit(solution)/shard_map/pmax | solution.py:82
  178.2 22.3 %all-reduce = (f32[2048]{0:T(1024)S(1)}, f32[2048]{0:T(1024)S(1)}) all-reduce(f32[2048]{0:T(1024)S(1)} %exponential_multiply_fusion, f32[2048]{0:T(1024)S(1)} %bitcast.89), channel_id=1, replica_groups=mesh['tower'=2,'narrow'=4,'wide'=4] {'tower','wide'}, use_global_device_ids=true, to_apply=%region_8.9 | all-reduce | flops 4096 | bytes 32768 | tf_op jit(solution)/shard_map/psum | solution.py:83
  200.5 0.6 fusion.54
  201.1 4.9 %while.27 = (s32[]{:T(128)}, f32[1024,256]{1,0:T(8,128)S(1)}, s32[4,1,256]{2,1,0:T(1,128)S(1)}, s32[4,512]{1,0:T(4,128)S(1)}, s32[4,512]{1,0:T(4,128)S(1)}, /*in...) while((s32[]{:T(128)}, f32[1024,256]{1,0:T(8,128)S(1)}, ...), condition=%wide.region_11.12_spmd.clone, body=%wide.region_10.11_spmd.clone.sunk | while | flops 542129152 | bytes 3177603 | solution.py:97
  201.2 1.2 fusion.75
  202.4 1.2 fusion.75
  203.7 1.2 fusion.75
  204.9 1.2 fusion.75
  206.1 1.1 broadcast_multiply_fusion
  207.1 0.0 reduce-scatter.2.cloned.1.call-update
  207.2 24.8 %reduce-scatter.2.cloned.1.call-done = f32[256,256]{1,0:T(8,128)} async-done(((f32[1024,256]{1,0:T(8,128)}), f32[256,256]{1,0:T(8,128)}) %reduce-scatter.2.cloned.1.call-update) | async-done | bytes 262160 | tf_op jit(solution)/shard_map/reduce_scatter | solution.py:102
  (37 shorter events, 0.5 us)
Async XLA Ops:
  7.2 85.9 %copy-start = (bf16[1024,256]{1,0:T(8,128)(2,1)S(1)}, bf16[1024,256]{1,0:T(8,128)(2,1)}, u32[]{:S(2)}) copy-start(bf16[1024,256]{1,0:T(8,128)(2,1)} %param.13) | copy-start | bytes 1572868
  7.2 85.9 %all-gather.2.cloned.1.call-start = ((), (), s32[]{:S(2)}) async-start(), calls=%async_computation.1 | async-start | bytes 5242880 | tf_op jit(solution)/shard_map/all_gather | solution.py:43
  7.9 145.4 %all-reduce.3.cloned.1.call-start = ((), (), s32[]{:S(2)}) async-start(), calls=%async_computation.2 | async-start | bytes 2097152 | tf_op jit(solution)/shard_map/psum | solution.py:52
  93.1 9.8 %copy-start.1 = (s32[1,1,256]{2,1,0:T(1,128)S(1)}, s32[1,1,256]{2,1,0:T(1,128)}, u32[]{:S(2)}) copy-start(s32[1,1,256]{2,1,0:T(1,128)} %param.15) | copy-start | bytes 3076
  102.7 53.5 %copy-start.2 = (bf16[2048,256]{1,0:T(8,128)(2,1)S(1)}, bf16[2048,256]{1,0:T(8,128)(2,1)}, u32[]{:S(2)}) copy-start(bf16[2048,256]{1,0:T(8,128)(2,1)} %param.14) | copy-start | bytes 3145732
  102.7 129.3 %reduce-scatter.2.cloned.1.call-start = ((), (), s32[]{:S(2)}) async-start(), calls=%async_computation.3 | async-start | bytes 1310720 | tf_op jit(solution)/shard_map/reduce_scatter | solution.py:102
Sparse Core Ops, SparseCore 0:
  9.6 83.4 all-gather.1
  102.9 50.3 all-reduce.2
  207.3 24.6 reduce-scatter.1
where the time goes:
time: 239 us
  waiting for transfers between devices  143 us (60%)
  blocking collectives  54.2 us (23%)
  matrix products  17 us (7%)
  between operations  13.9 us (6%)
  other arithmetic  8.95 us (4%)
    all_gather x1, waiting for transfers between devices, local(): lax.all_gather(features, 'narrow', axis=0, tiled=True)  85.1 us
    psum x1, waiting for transfers between devices, local(): item_vec = unit_rows(lax.psum(partial_embed, 'narrow')).astype(jnp.bfloat16)  32.6 us
    reduce_scatter x1, waiting for transfers between devices, local(): lax.psum_scatter(INV_TEMP * acc, 'narrow', scatter_dimension=0, tiled=True)  24.8 us
    psum x1, blocking collectives, local(): lax.psum((mass * jnp.exp(top - global_top), pos), ('tower', 'wide'))  22.3 us
    pmax x1, blocking collectives, local(): global_top = lax.pmax(top, ('tower', 'wide'))  14.1 us
    dot_general x1, matrix products, local(): partial_embed = jnp.dot(hidden, w_out, preferred_element_type=jnp.float32)  9.62 us
    all_gather x1, blocking collectives, local(): lax.all_gather(item_ids, ('tower', 'wide'), axis=1, tiled=True)  9.02 us
    all_gather x1, blocking collectives, local(): lax.all_gather(item_ids, 'narrow', axis=0, tiled=True)  8.76 us
  transfers between devices with their start and end apart: 3, of which 3 were waited for; matrix products, arithmetic and copies ran while one was open for 0% of the time, Pallas kernels for 0%

commit v1 on v0

--- a/solution.py
+++ b/solution.py
@@ -80,7 +80,7 @@
     mass = mass.reshape(users_dev)
     pos = pos.reshape(users_dev)
     global_top = lax.pmax(top, ("tower", "wide"))
-    total, global_pos = lax.psum((mass * jnp.exp(top - global_top), pos), ("tower", "wide"))
+    total, global_pos = lax.psum(lax.psum((mass * jnp.exp(top - global_top), pos), "wide"), "tower")
     lse = global_top + jnp.log(total)
     row_loss = lse - global_pos
     lse_blocks = lse.reshape(count, block)

time: 239 us -> 235 us (0.983)
  blocking collectives: 54.2 us -> 49.1 us
    psum x1 -> x2, blocking collectives: 22.3 us -> 17.3 us  [the longest x1 10.1 us: local(): lax.psum((mass * jnp.exp(top - global_top), pos), 'wide')]
where the time goes in v1:
time: 235 us; the launch traced here: 234 us
  waiting for transfers between devices  144 us (61%)
  blocking collectives  49.1 us (21%)
  matrix products  17 us (7%)
  between operations  13.9 us (6%)
  other arithmetic  8.95 us (4%)
    all_gather x1, waiting for transfers between devices, local(): lax.all_gather(features, 'narrow', axis=0, tiled=True)  85.1 us
    psum x1, waiting for transfers between devices, local(): item_vec = unit_rows(lax.psum(partial_embed, 'narrow')).astype(jnp.bfloat16)  32.6 us
    reduce_scatter x1, waiting for transfers between devices, local(): lax.psum_scatter(INV_TEMP * acc, 'narrow', scatter_dimension=0, tiled=True)  25.7 us
    pmax x1, blocking collectives, local(): global_top = lax.pmax(top, ('tower', 'wide'))  14.1 us
    psum x1, blocking collectives, local(): lax.psum((mass * jnp.exp(top - global_top), pos), 'wide')  10.1 us
    dot_general x1, matrix products, local(): partial_embed = jnp.dot(hidden, w_out, preferred_element_type=jnp.float32)  9.62 us
    all_gather x1, blocking collectives, local(): lax.all_gather(item_ids, ('tower', 'wide'), axis=1, tiled=True)  9.02 us
    all_gather x1, blocking collectives, local(): lax.all_gather(item_ids, 'narrow', axis=0, tiled=True)  8.76 us
  transfers between devices with their start and end apart: 3, of which 3 were waited for; matrix products, arithmetic and copies ran while one was open for 0% of the time, Pallas kernels for 0%

profile of v1, /device:TPU:0, one launch (start us, length us, event | category | flops | bytes accessed | tf_op | source)
XLA Modules:
  0.0 234.3 jit_solution(12220538595648621567)
XLA Ops:
  7.2 0.0 copy-start
  7.2 0.0 all-gather.2.cloned.1.call-start
  7.2 0.7 all-gather.2.cloned.1.call-update
  7.9 0.0 all-reduce.4.cloned.1.call-start
  8.0 85.1 %all-gather.2.cloned.1.call-done = bf16[4,1,256,2048]{3,2,1,0:T(8,128)(2,1)} async-done(((bf16[1,1,256,2048]{3,2,1,0:T(8,128)(2,1)}), bf16[4,1,256,2048]{3,2,1,0:T(8,128)(2,1)}) %all-gather.2.cloned.1.call-update) | async-done | bytes 4194320 | tf_op jit(solution)/shard_map/all_gather | solution.py:43
  93.1 0.0 copy-done
  93.1 0.0 copy-start.1
  93.1 9.6 %fusion.48 = f32[1024,256]{1,0:T(8,128)} fusion(bf16[1024,256]{1,0:T(8,128)(2,1)S(1)} %copy-done, f32[1024]{0:T(1024)} %param.12, bf16[1024,2048]{1,0:T(8,128)(2,1)} %bitcast.95, bf16[2048,1024]{1,0:T(8,128)(2,1)} %param.11), kind=kOutput, calls=%fused_computation.64 | convolution fusion | flops 4834983936 | bytes 9965568 | tf_op jit(solution)/shard_map/dot_general | solution.py:51
  102.7 0.0 copy-start.2
  102.7 0.0 all-reduce.4.cloned.1.call-update
  102.7 0.0 reduce-scatter.2.cloned.1.call-start
  102.8 0.0 copy-done.1
  102.8 9.0 %all_gather.9 = s32[1,8,256]{2,0,1:T(1,128)S(1)} all-gather(s32[1,1,256]{2,0,1:T(1,128)S(1)} %bitcast.94), channel_id=1, replica_groups=mesh['tower'=2,'narrow'=4,'wide'=4] {'tower','wide'}, dimensions={1}, use_global_device_ids=true | all-gather | bytes 9216 | tf_op jit(solution)/shard_map/all_gather | solution.py:53
  111.9 8.8 %all_gather.10 = s32[4,1,256]{2,1,0:T(1,128)S(1)} all-gather(s32[1,1,256]{2,1,0:T(1,128)S(1)} %copy-done.1), channel_id=1, replica_groups=mesh['tower'=2,'narrow'=4,'wide'=4] {'narrow'}, dimensions={0}, use_global_device_ids=true | all-gather | bytes 5120 | tf_op jit(solution)/shard_map/all_gather | solution.py:44
  120.7 32.6 %all-reduce.4.cloned.1.call-done = f32[1024,256]{1,0:T(8,128)} async-done(((f32[1024,256]{1,0:T(8,128)}), f32[1024,256]{1,0:T(8,128)}) %all-reduce.4.cloned.1.call-update) | async-done | bytes 1048592 | tf_op jit(solution)/shard_map/psum | solution.py:52
  153.3 1.4 multiply_reduce_fusion
  154.8 1.4 multiply_convert_fusion
  156.2 0.0 copy-done.2
  156.2 7.8 %while.26 = (s32[]{:T(128)}, f32[4,512]{1,0:T(4,128)S(1)}, f32[4,512]{1,0:T(4,128)S(1)}, f32[4,512]{1,0:T(4,128)S(1)}, s32[4,512]{1,0:T(4,128)S(1)}, /*index=5*/...) while((s32[]{:T(128)}, f32[4,512]{1,0:T(4,128)S(1)}, ...), condition=%wide.region_6.7_spmd.clone, body=%wide.region_2.6_spmd.clone.sunk | while | flops 276313600 | bytes 5038221 | solution.py:78
  156.2 0.7 select_reduce_fusion.3
  156.9 1.1 fusion.70
  158.0 0.1 dynamic_update_slice.17
  158.1 0.1 dynamic_update_slice.16
  158.2 0.7 select_reduce_fusion.3
  158.9 1.1 fusion.70
  160.0 0.1 dynamic_update_slice.17
  160.0 0.1 dynamic_update_slice.16
  160.1 0.7 select_reduce_fusion.3
  160.8 1.1 fusion.70
  161.9 0.1 dynamic_update_slice.17
  162.0 0.1 dynamic_update_slice.16
  162.1 0.7 select_reduce_fusion.3
  162.8 1.1 fusion.70
  163.9 0.1 dynamic_update_slice.17
  164.0 0.1 dynamic_update_slice.16
  164.0 14.1 %pmax.7 = f32[2048]{0:T(1024)S(1)} all-reduce(f32[2048]{0:T(1024)S(1)} %bitcast.84), channel_id=1, replica_groups=mesh['tower'=2,'narrow'=4,'wide'=4] {'tower','wide'}, use_global_device_ids=true, to_apply=%region_7.8 | all-reduce | flops 2048 | bytes 16384 | tf_op jit(solution)/shard_map/pmax | solution.py:82
  178.2 10.1 %all-reduce = (f32[2048]{0:T(1024)S(1)}, f32[2048]{0:T(1024)S(1)}) all-reduce(f32[2048]{0:T(1024)S(1)} %exponential_multiply_fusion, f32[2048]{0:T(1024)S(1)} %bitcast.89), channel_id=1, replica_groups=mesh['tower'=2,'narrow'=4,'wide'=4] {'wide'}, use_global_device_ids=true, to_apply=%region_8.9 | all-reduce | flops 4096 | bytes 32768 | tf_op jit(solution)/shard_map/psum | solution.py:83
  188.3 7.1 %all-reduce.1 = (f32[2048]{0:T(1024)S(1)}, f32[2048]{0:T(1024)S(1)}) all-reduce(f32[2048]{0:T(1024)S(1)} %get-tuple-element.203, f32[2048]{0:T(1024)S(1)} %get-tuple-element.204), channel_id=1, replica_groups=mesh['tower'=2,'narrow'=4,'wide'=4] {'tower'}, use_global_device_ids=true, to_apply=%region_9.10 | all-reduce | flops 4096 | bytes 32768 | tf_op jit(solution)/shard_map/psum | solution.py:83
  195.4 0.6 fusion.54
  196.1 4.9 %while.27 = (s32[]{:T(128)}, f32[1024,256]{1,0:T(8,128)S(1)}, s32[4,1,256]{2,1,0:T(1,128)S(1)}, s32[4,512]{1,0:T(4,128)S(1)}, s32[4,512]{1,0:T(4,128)S(1)}, /*in...) while((s32[]{:T(128)}, f32[1024,256]{1,0:T(8,128)S(1)}, ...), condition=%wide.region_13.14_spmd.clone, body=%wide.region_12.13_spmd.clone.sunk | while | flops 542129152 | bytes 3177603 | solution.py:97
  196.1 1.2 fusion.75
  197.3 1.2 fusion.75
  198.6 1.2 fusion.75
  199.8 1.2 fusion.75
  201.0 1.1 broadcast_multiply_fusion
  202.1 0.0 reduce-scatter.2.cloned.1.call-update
  202.1 25.7 %reduce-scatter.2.cloned.1.call-done = f32[256,256]{1,0:T(8,128)} async-done(((f32[1024,256]{1,0:T(8,128)}), f32[256,256]{1,0:T(8,128)}) %reduce-scatter.2.cloned.1.call-update) | async-done | bytes 262160 | tf_op jit(solution)/shard_map/reduce_scatter | solution.py:102
  (37 shorter events, 0.5 us)
Async XLA Ops:
  7.2 85.9 %copy-start = (bf16[1024,256]{1,0:T(8,128)(2,1)S(1)}, bf16[1024,256]{1,0:T(8,128)(2,1)}, u32[]{:S(2)}) copy-start(bf16[1024,256]{1,0:T(8,128)(2,1)} %param.13) | copy-start | bytes 1572868
  7.2 85.9 %all-gather.2.cloned.1.call-start = ((), (), s32[]{:S(2)}) async-start(), calls=%async_computation.1 | async-start | bytes 5242880 | tf_op jit(solution)/shard_map/all_gather | solution.py:43
  7.9 145.4 %all-reduce.4.cloned.1.call-start = ((), (), s32[]{:S(2)}) async-start(), calls=%async_computation.2 | async-start | bytes 2097152 | tf_op jit(solution)/shard_map/psum | solution.py:52
  93.1 9.8 %copy-start.1 = (s32[1,1,256]{2,1,0:T(1,128)S(1)}, s32[1,1,256]{2,1,0:T(1,128)}, u32[]{:S(2)}) copy-start(s32[1,1,256]{2,1,0:T(1,128)} %param.15) | copy-start | bytes 3076
  102.7 53.5 %copy-start.2 = (bf16[2048,256]{1,0:T(8,128)(2,1)S(1)}, bf16[2048,256]{1,0:T(8,128)(2,1)}, u32[]{:S(2)}) copy-start(bf16[2048,256]{1,0:T(8,128)(2,1)} %param.14) | copy-start | bytes 3145732
  102.7 125.1 %reduce-scatter.2.cloned.1.call-start = ((), (), s32[]{:S(2)}) async-start(), calls=%async_computation.3 | async-start | bytes 1310720 | tf_op jit(solution)/shard_map/reduce_scatter | solution.py:102
Sparse Core Ops, SparseCore 0:
  9.6 83.4 all-gather.1
  102.9 50.3 all-reduce.3
  202.2 25.5 reduce-scatter.1
